TPU v7x, 256 devices: a whole 4x4x8 slice. The times are simulated.
256 devices in a mesh: section: 4 (over x_hi, core), dp: 64 (over x_lo, y, z).
Axes of the slice: x: 4 (x_hi: 2, x_lo: 2; x = x_hi * 2 + x_lo), y: 4, z: 8, core: 2. Of those that a mesh axis runs over, the one named last changes fastest.
Arguments:
- currents: bfloat16 [2, 2, 8192, 1024], P(None, None, 'dp'), may hold values from -6 to 6
- weights: bfloat16 [2, 4, 1024, 1024], P(None, 'section'), may hold values from -0.1875 to 0.1875
- decay: float32 [2, 4, 1024], P(None, 'section'), may hold values from 0.2 to 0.95
- out_grad: bfloat16 [2, 2, 8192, 1024], P(None, None, 'dp'), may hold values from -0.09375 to 0.09375
Outputs:
- grad_weights: bfloat16 [2, 4, 1024, 1024], P(None, 'section', 'dp')
- grad_decay: float32 [2, 4, 1024], P(None, 'section', 'dp')
All inputs are finite; a program needn't handle non-finite values.
Results may differ from a plain program's by a relative error of at most 0.018.
The roundings to bfloat16 on the way count: a program that leaves them out, or rounds other values in their place, can miss the bound.
Values may be sent and summed in bfloat16 or wider, within the bound.
A program may use at most 128 MiB of HBM per device.

v0:
```python
import jax
import jax.numpy as jnp
from jax import lax
from jax.sharding import PartitionSpec as P

spike_gain = 4.0


def from_behind(x, axis, by):
    length = lax.axis_size(axis)
    return lax.ppermute(x, axis, [(i, (i + by) % length) for i in range(length)])


def for_sending(x):

    def short(part):
        return part.astype(jnp.bfloat16) if part.dtype == jnp.float32 else part

    return jax.tree.map(short, x)


def membranes(section_in, weight, decay_rate):
    result = []
    voltage = None
    for instant in range(section_in.shape[0]):
        pre = jnp.dot(section_in[instant], weight, preferred_element_type=jnp.float32)
        if instant == 0:
            level = pre
        else:
            level = decay_rate * voltage + pre
        spikes = jax.nn.sigmoid(spike_gain * (level - 1.0))
        voltage = level * (1.0 - spikes)
        result.append(level)
    return jnp.stack(result)


def backward_section(section_in, membrane, incoming, weight, decay_rate):
    spikes = jax.nn.sigmoid(spike_gain * (membrane - 1.0))
    voltage = membrane * (1.0 - spikes)
    spike_slope = spike_gain * spikes * (1.0 - spikes)
    keep_slope = 1.0 - spikes - membrane * spike_slope
    step_count = section_in.shape[0]
    carried = jnp.zeros(membrane.shape[1:], jnp.float32)
    dweight = jnp.zeros((weight.shape[0], weight.shape[1]), jnp.float32)
    ddecay = jnp.zeros((weight.shape[1],), jnp.float32)
    results = [None] * step_count
    for instant in reversed(range(step_count)):
        grad_h = (
            incoming[instant].astype(jnp.float32) * spike_slope[instant]
            + carried * keep_slope[instant]
        )
        grad_round = grad_h.astype(jnp.bfloat16)
        dweight = dweight + lax.dot_general(
            section_in[instant],
            grad_round,
            (((0,), (0,)), ((), ())),
            preferred_element_type=jnp.float32,
        )
        back = lax.dot_general(
            grad_round, weight, (((1,), (1,)), ((), ())), preferred_element_type=jnp.float32
        )
        results[instant] = (incoming[instant].astype(jnp.float32) + back).astype(jnp.bfloat16)
        if instant > 0:
            ddecay = ddecay + jnp.sum(grad_h * voltage[instant - 1], axis=0)
        carried = decay_rate * grad_h
    return (jnp.stack(results), dweight, ddecay)


def on_device(currents, weights, decay, out_grad):
    sections = lax.axis_size("section")
    position = lax.axis_index("section")
    micro_count, step_count, rows_here, channels = currents.shape
    own_weights = weights[:, 0]
    own_decay = decay[:, 0]
    tick_count = 2 * sections + micro_count - 1
    saved_inputs = jnp.zeros((2, micro_count, step_count, rows_here, channels), jnp.bfloat16)
    states = jnp.zeros((1,), jnp.float32)
    arriving = jnp.zeros((step_count, rows_here, channels), jnp.bfloat16)

    def forward_tick(moment, loop_state):
        arriving, saved_inputs, states = loop_state
        offset = moment - position
        circuit = (offset >= sections).astype(jnp.int32)
        batch_slot = offset - circuit * sections
        active_now = (offset >= 0) & (batch_slot < micro_count)
        slot = jnp.clip(batch_slot, 0, micro_count - 1)
        fresh_in = lax.dynamic_index_in_dim(currents, slot, 0, keepdims=False)
        section_in = jnp.where((position == 0) & (circuit == 0), fresh_in, arriving)

        def forward_working(operands):
            section_in, saved_inputs, states = operands
            weight = lax.dynamic_index_in_dim(own_weights, circuit, 0, keepdims=False)
            decay_rate = lax.dynamic_index_in_dim(own_decay, circuit, 0, keepdims=False)
            membrane = membranes(section_in, weight, decay_rate)
            spikes = jax.nn.sigmoid(spike_gain * (membrane - 1.0))
            section_out = (section_in.astype(jnp.float32) + spikes).astype(jnp.bfloat16)
            saved_inputs = saved_inputs.at[circuit, slot].set(section_in)
            return (section_out, saved_inputs, states)

        def forward_resting(operands):
            return (jnp.zeros_like(operands[0]), operands[1], operands[2])

        section_out, saved_inputs, states = lax.cond(
            active_now, forward_working, forward_resting, (section_in, saved_inputs, states)
        )
        arriving = from_behind(section_out, "section", 1)
        return (arriving, saved_inputs, states)

    arriving, saved_inputs, states = lax.fori_loop(
        0, tick_count, forward_tick, (arriving, saved_inputs, states)
    )

    def backward_tick(moment, loop_state):
        arriving, grad_w, grad_d = loop_state
        offset = moment - (sections - 1 - position)
        circuit = jnp.where(offset >= sections, 0, 1).astype(jnp.int32)
        batch_slot = offset - (1 - circuit) * sections
        active_now = (offset >= 0) & (batch_slot < micro_count)
        slot = jnp.clip(batch_slot, 0, micro_count - 1)
        fresh_in = lax.dynamic_index_in_dim(out_grad, slot, 0, keepdims=False)
        incoming = jnp.where((position == sections - 1) & (circuit == 1), fresh_in, arriving)

        def backward_working(operands):
            incoming, grad_w, grad_d = operands
            weight = lax.dynamic_index_in_dim(own_weights, circuit, 0, keepdims=False)
            decay_rate = lax.dynamic_index_in_dim(own_decay, circuit, 0, keepdims=False)
            section_in = saved_inputs[circuit, slot]
            membrane = membranes(section_in, weight, decay_rate)
            back_out, dweight, ddecay = backward_section(
                section_in, membrane, incoming, weight, decay_rate
            )
            grad_w = grad_w.at[circuit].add(dweight)
            grad_d = grad_d.at[circuit].add(ddecay)
            return (back_out, grad_w, grad_d)

        def backward_resting(operands):
            return (jnp.zeros_like(operands[0]), operands[1], operands[2])

        back_out, grad_w, grad_d = lax.cond(
            active_now, backward_working, backward_resting, (incoming, grad_w, grad_d)
        )
        arriving = from_behind(for_sending(back_out), "section", -1).astype(back_out.dtype)
        return (arriving, grad_w, grad_d)

    grad_w = jnp.zeros((2, channels, channels), jnp.float32)
    grad_d = jnp.zeros((2, channels), jnp.float32)
    arriving = jnp.zeros((step_count, rows_here, channels), jnp.bfloat16)
    middle = sections + micro_count - 1
    arriving, grad_w, grad_d = lax.fori_loop(0, middle, backward_tick, (arriving, grad_w, grad_d))
    arriving, grad_w, grad_d = lax.fori_loop(
        middle, tick_count, backward_tick, (arriving, grad_w, grad_d)
    )
    summed_w, summed_d = (
        lax.psum_scatter(grad_w, "dp", scatter_dimension=1, tiled=True),
        lax.psum_scatter(grad_d, "dp", scatter_dimension=1, tiled=True),
    )
    return (summed_w.astype(jnp.bfloat16)[:, None], summed_d[:, None])


def solution(mesh):
    in_specs = (
        P(None, None, "dp", None),
        P(None, "section", None, None),
        P(None, "section", None),
        P(None, None, "dp", None),
    )
    out_specs = (P(None, "section", "dp", None), P(None, "section", "dp"))
    return jax.shard_map(
        on_device, mesh=mesh, in_specs=in_specs, out_specs=out_specs, check_vma=False
    )
```

profile of v0, /device:TPU:2, one launch (start us, length us, event | category | flops | bytes accessed | tf_op | source)
XLA Modules:
  0.0 1027.7 jit_solution(12376369421322190573)
XLA Ops:
  8.2 125.4 %while.62 = (s32[]{:T(128)}, bf16[2,128,1024]{2,1,0:T(8,128)(2,1)S(1)}, bf16[2,2,2,128,1024]{4,3,2,1,0:T(8,128)(2,1)S(1)}, s32[]{:T(128)}, pred[]{:T(512)}, /*in...) while((s32[]{:T(128)}, ...), condition=%wide.region_4.5_spmd, body=%wide.region_0.4_spmd.sunk | while | flops 540934144 | bytes 29897724 | solution.py:109
  8.3 6.5 conditional.6
  14.9 10.1 collective-permute-done
  25.0 6.5 conditional.6
  31.6 10.1 collective-permute-done
  41.8 10.1 collective-permute-done
  52.1 12.5 %collective-permute-done = bf16[2,128,1024]{2,1,0:T(8,128)(2,1)S(1)} collective-permute-done((bf16[2,128,1024]{2,1,0:T(8,128)(2,1)S(1)}, bf16[2,128,1024]{2,1,0:T(8,128)(2,1)S(1)}, u32[]{:S(2)}, u32[]{:S(2)}) %collective-permute-start) | collective-permute-done | bytes 524320 | tf_op jit(solution)/shard_map/while/body/eval_jaxpr/ppermute | solution.py:11
  64.6 6.5 conditional.6
  71.2 10.1 collective-permute-done
  81.3 6.5 conditional.6
  87.9 10.1 collective-permute-done
  98.2 10.1 collective-permute-done
  108.4 12.5 %collective-permute-done = bf16[2,128,1024]{2,1,0:T(8,128)(2,1)S(1)} collective-permute-done((bf16[2,128,1024]{2,1,0:T(8,128)(2,1)S(1)}, bf16[2,128,1024]{2,1,0:T(8,128)(2,1)S(1)}, u32[]{:S(2)}, u32[]{:S(2)}) %collective-permute-start) | collective-permute-done | bytes 524320 | tf_op jit(solution)/shard_map/while/body/eval_jaxpr/ppermute | solution.py:11
  121.1 12.5 %collective-permute-done = bf16[2,128,1024]{2,1,0:T(8,128)(2,1)S(1)} collective-permute-done((bf16[2,128,1024]{2,1,0:T(8,128)(2,1)S(1)}, bf16[2,128,1024]{2,1,0:T(8,128)(2,1)S(1)}, u32[]{:S(2)}, u32[]{:S(2)}) %collective-permute-start) | collective-permute-done | bytes 524320 | tf_op jit(solution)/shard_map/while/body/eval_jaxpr/ppermute | solution.py:11
  133.7 4.3 broadcast_in_dim.59
  138.0 130.3 %while.63 = (s32[]{:T(128)}, bf16[2,128,1024]{2,1,0:T(8,128)(2,1)S(1)}, f32[2,1024,1024]{2,1,0:T(8,128)}, f32[2,1024]{1,0:T(2,128)S(1)}, s32[]{:T(128)}, /*index...) while((s32[]{:T(128)}, ...), condition=%wide.region_11.12_spmd, body=%wide.region_5.11_spmd.sunk | while | flops 1621623808 | bytes 61649988 | solution.py:149
  138.9 18.9 %collective-permute-start.1 = (bf16[2,128,1024]{2,1,0:T(8,128)(2,1)}, bf16[2,128,1024]{2,1,0:T(8,128)(2,1)S(1)}, u32[]{:S(2)}, u32[]{:S(2)}) collective-permute-start(bf16[2,128,1024]{2,1,0:T(8,128)(2,1)} %get-tuple-element.1199), channel_id=1, source_target_pairs={{0,192},{64,0},{128,64},{192,128},{1,193},{65,1},{129,65},{193,129... | collective-permute-start | bytes 1572872 | tf_op jit(solution)/shard_map/while/body/eval_jaxpr/ppermute | solution.py:11
  157.8 7.0 collective-permute-done.1
  165.8 23.0 %collective-permute-start.1 = (bf16[2,128,1024]{2,1,0:T(8,128)(2,1)}, bf16[2,128,1024]{2,1,0:T(8,128)(2,1)S(1)}, u32[]{:S(2)}, u32[]{:S(2)}) collective-permute-start(bf16[2,128,1024]{2,1,0:T(8,128)(2,1)} %get-tuple-element.1199), channel_id=1, source_target_pairs={{0,192},{64,0},{128,64},{192,128},{1,193},{65,1},{129,65},{193,129... | collective-permute-start | bytes 1572872 | tf_op jit(solution)/shard_map/while/body/eval_jaxpr/ppermute | solution.py:11
  188.8 7.0 collective-permute-done.1
  196.7 3.3 collective-permute-start.1
  200.0 9.8 collective-permute-done.1
  209.8 20.6 %conditional.7 = (bf16[2,128,1024]{2,1,0:T(8,128)(2,1)}, f32[2,1024,1024]{2,1,0:T(8,128)}, f32[2,1024]{1,0:T(2,128)S(1)}) conditional(s32[]{:T(128)} %convert_element_type.265, (f32[2,1024,1024]{2,1,0:T(8,128)}, f32[2,1024]{1,0:T(2,128)S(1)}) %tuple.173, (s32[]{:T(128)}, pred[]{:T(512)}, s32[]{:T(128)}, bf16[2,2,128,1024]{3,2,1,0:T(8,128)(2,1)}, ...), branch_computations={%region_6.6_spmd, %region_7.10_spmd} | conditional | flops 1621623808 | bytes 59552472 | solution.py:139
  218.2 2.4 fusion.53
  220.6 2.4 fusion.56
  224.7 5.7 fusion.22
  230.4 10.3 %collective-permute-done.1 = bf16[2,128,1024]{2,1,0:T(8,128)(2,1)S(1)} collective-permute-done((bf16[2,128,1024]{2,1,0:T(8,128)(2,1)}, bf16[2,128,1024]{2,1,0:T(8,128)(2,1)S(1)}, u32[]{:S(2)}, u32[]{:S(2)}) %collective-permute-start.1) | collective-permute-done | bytes 524320 | tf_op jit(solution)/shard_map/while/body/eval_jaxpr/ppermute | solution.py:11
  240.7 20.6 %conditional.7 = (bf16[2,128,1024]{2,1,0:T(8,128)(2,1)}, f32[2,1024,1024]{2,1,0:T(8,128)}, f32[2,1024]{1,0:T(2,128)S(1)}) conditional(s32[]{:T(128)} %convert_element_type.265, (f32[2,1024,1024]{2,1,0:T(8,128)}, f32[2,1024]{1,0:T(2,128)S(1)}) %tuple.173, (s32[]{:T(128)}, pred[]{:T(512)}, s32[]{:T(128)}, bf16[2,2,128,1024]{3,2,1,0:T(8,128)(2,1)}, ...), branch_computations={%region_6.6_spmd, %region_7.10_spmd} | conditional | flops 1621623808 | bytes 59552472 | solution.py:139
  249.1 2.4 fusion.53
  251.6 2.4 fusion.56
  255.6 5.7 fusion.22
  261.3 7.0 collective-permute-done.1
  268.3 102.9 %while.64 = (s32[]{:T(128)}, bf16[2,128,1024]{2,1,0:T(8,128)(2,1)S(1)}, f32[2,1024,1024]{2,1,0:T(8,128)}, f32[2,1024]{1,0:T(2,128)S(1)}, s32[]{:T(128)}, /*index...) while((s32[]{:T(128)}, ...), condition=%wide.region_18.19_spmd, body=%wide.region_12.18_spmd.sunk | while | flops 1621623808 | bytes 61650008 | solution.py:150
  269.2 22.8 %collective-permute-start.2 = (bf16[2,128,1024]{2,1,0:T(8,128)(2,1)}, bf16[2,128,1024]{2,1,0:T(8,128)(2,1)S(1)}, u32[]{:S(2)}, u32[]{:S(2)}) collective-permute-start(bf16[2,128,1024]{2,1,0:T(8,128)(2,1)} %get-tuple-element.1212), channel_id=1, source_target_pairs={{0,192},{64,0},{128,64},{192,128},{1,193},{65,1},{129,65},{193,129... | collective-permute-start | bytes 1572872 | tf_op jit(solution)/shard_map/while/body/eval_jaxpr/ppermute | solution.py:11
  292.1 7.0 collective-permute-done.2
  300.0 3.3 collective-permute-start.2
  303.3 9.7 collective-permute-done.2
  313.0 20.4 %conditional.8 = (bf16[2,128,1024]{2,1,0:T(8,128)(2,1)}, f32[2,1024,1024]{2,1,0:T(8,128)}, f32[2,1024]{1,0:T(2,128)S(1)}) conditional(s32[]{:T(128)} %convert_element_type.266, (f32[2,1024,1024]{2,1,0:T(8,128)}, f32[2,1024]{1,0:T(2,128)S(1)}) %tuple.176, (s32[]{:T(128)}, pred[]{:T(512)}, s32[]{:T(128)}, bf16[2,2,128,1024]{3,2,1,0:T(8,128)(2,1)}, ...), branch_computations={%region_13.13_spmd, %region_14.17_spmd} | conditional | flops 1621623808 | bytes 59552472 | solution.py:139
  321.3 2.4 fusion.112
  323.7 2.4 fusion.115
  327.8 5.6 fusion.81
  333.4 10.3 %collective-permute-done.2 = bf16[2,128,1024]{2,1,0:T(8,128)(2,1)S(1)} collective-permute-done((bf16[2,128,1024]{2,1,0:T(8,128)(2,1)}, bf16[2,128,1024]{2,1,0:T(8,128)(2,1)S(1)}, u32[]{:S(2)}, u32[]{:S(2)}) %collective-permute-start.2) | collective-permute-done | bytes 524320 | tf_op jit(solution)/shard_map/while/body/eval_jaxpr/ppermute | solution.py:11
  343.8 20.4 %conditional.8 = (bf16[2,128,1024]{2,1,0:T(8,128)(2,1)}, f32[2,1024,1024]{2,1,0:T(8,128)}, f32[2,1024]{1,0:T(2,128)S(1)}) conditional(s32[]{:T(128)} %convert_element_type.266, (f32[2,1024,1024]{2,1,0:T(8,128)}, f32[2,1024]{1,0:T(2,128)S(1)}) %tuple.176, (s32[]{:T(128)}, pred[]{:T(512)}, s32[]{:T(128)}, bf16[2,2,128,1024]{3,2,1,0:T(8,128)(2,1)}, ...), branch_computations={%region_13.13_spmd, %region_14.17_spmd} | conditional | flops 1621623808 | bytes 59552472 | solution.py:139
  354.5 2.4 fusion.115
  358.6 5.6 fusion.81
  364.2 7.0 collective-permute-done.2
  373.1 316.9 %reduce-scatter.7.cloned.1.call-done = f32[16,2]{1,0:T(8,128)} async-done(((f32[1024,2]{1,0:T(8,128)}), f32[16,2]{1,0:T(8,128)}) %reduce-scatter.7.cloned.1.call-update) | async-done | bytes 144
  691.3 328.1 %reduce-scatter.5.cloned.1.call-done = f32[2,16,1024]{2,1,0:T(8,128)} async-done(((f32[2,1024,1024]{2,1,0:T(8,128)}), f32[2,16,1024]{2,1,0:T(8,128)}) %reduce-scatter.5.cloned.1.call-update) | async-done | bytes 131088 | tf_op jit(solution)/shard_map/reduce_scatter | solution.py:154
  (142 shorter events, 84.3 us)
Async XLA Ops:
  7.2 682.8 %reduce-scatter.7.cloned.1.call-start = ((), (), s32[]{:S(2)}) async-start(), calls=%async_computation.3 | async-start | bytes 532480
  8.4 5.5 copy-start
  14.8 10.2 collective-permute-start
  25.1 5.5 copy-start
  31.5 10.2 collective-permute-start
  41.7 10.2 collective-permute-start
  52.0 12.6 %collective-permute-start = (bf16[2,128,1024]{2,1,0:T(8,128)(2,1)S(1)}, bf16[2,128,1024]{2,1,0:T(8,128)(2,1)S(1)}, u32[]{:S(2)}, u32[]{:S(2)}) collective-permute-start(bf16[2,128,1024]{2,1,0:T(8,128)(2,1)S(1)} %get-tuple-element.1187), channel_id=1, source_target_pairs={{0,64},{64,128},{128,192},{192,0},{1,65},{65,129},{129,193},{193,1... | collective-permute-start | bytes 1572872 | tf_op jit(solution)/shard_map/while/body/eval_jaxpr/ppermute | solution.py:11
  64.7 5.5 copy-start
  71.1 10.2 collective-permute-start
  81.4 5.5 copy-start
  87.8 10.2 collective-permute-start
  98.1 10.2 collective-permute-start
  108.3 12.6 %collective-permute-start = (bf16[2,128,1024]{2,1,0:T(8,128)(2,1)S(1)}, bf16[2,128,1024]{2,1,0:T(8,128)(2,1)S(1)}, u32[]{:S(2)}, u32[]{:S(2)}) collective-permute-start(bf16[2,128,1024]{2,1,0:T(8,128)(2,1)S(1)} %get-tuple-element.1187), channel_id=1, source_target_pairs={{0,64},{64,128},{128,192},{192,0},{1,65},{65,129},{129,193},{193,1... | collective-permute-start | bytes 1572872 | tf_op jit(solution)/shard_map/while/body/eval_jaxpr/ppermute | solution.py:11
  121.0 12.6 %collective-permute-start = (bf16[2,128,1024]{2,1,0:T(8,128)(2,1)S(1)}, bf16[2,128,1024]{2,1,0:T(8,128)(2,1)S(1)}, u32[]{:S(2)}, u32[]{:S(2)}) collective-permute-start(bf16[2,128,1024]{2,1,0:T(8,128)(2,1)S(1)} %get-tuple-element.1187), channel_id=1, source_target_pairs={{0,64},{64,128},{128,192},{192,0},{1,65},{65,129},{129,193},{193,1... | collective-permute-start | bytes 1572872 | tf_op jit(solution)/shard_map/while/body/eval_jaxpr/ppermute | solution.py:11
  138.9 26.0 %collective-permute-start.1 = (bf16[2,128,1024]{2,1,0:T(8,128)(2,1)}, bf16[2,128,1024]{2,1,0:T(8,128)(2,1)S(1)}, u32[]{:S(2)}, u32[]{:S(2)}) collective-permute-start(bf16[2,128,1024]{2,1,0:T(8,128)(2,1)} %get-tuple-element.1199), channel_id=1, source_target_pairs={{0,192},{64,0},{128,64},{192,128},{1,193},{65,1},{129,65},{193,129... | collective-permute-start | bytes 1572872 | tf_op jit(solution)/shard_map/while/body/eval_jaxpr/ppermute | solution.py:11
  165.8 30.0 %collective-permute-start.1 = (bf16[2,128,1024]{2,1,0:T(8,128)(2,1)}, bf16[2,128,1024]{2,1,0:T(8,128)(2,1)S(1)}, u32[]{:S(2)}, u32[]{:S(2)}) collective-permute-start(bf16[2,128,1024]{2,1,0:T(8,128)(2,1)} %get-tuple-element.1199), channel_id=1, source_target_pairs={{0,192},{64,0},{128,64},{192,128},{1,193},{65,1},{129,65},{193,129... | collective-permute-start | bytes 1572872 | tf_op jit(solution)/shard_map/while/body/eval_jaxpr/ppermute | solution.py:11
  196.7 13.1 %collective-permute-start.1 = (bf16[2,128,1024]{2,1,0:T(8,128)(2,1)}, bf16[2,128,1024]{2,1,0:T(8,128)(2,1)S(1)}, u32[]{:S(2)}, u32[]{:S(2)}) collective-permute-start(bf16[2,128,1024]{2,1,0:T(8,128)(2,1)} %get-tuple-element.1199), channel_id=1, source_target_pairs={{0,192},{64,0},{128,64},{192,128},{1,193},{65,1},{129,65},{193,129... | collective-permute-start | bytes 1572872 | tf_op jit(solution)/shard_map/while/body/eval_jaxpr/ppermute | solution.py:11
  209.8 6.1 copy-start.1
  230.4 10.3 %collective-permute-start.1 = (bf16[2,128,1024]{2,1,0:T(8,128)(2,1)}, bf16[2,128,1024]{2,1,0:T(8,128)(2,1)S(1)}, u32[]{:S(2)}, u32[]{:S(2)}) collective-permute-start(bf16[2,128,1024]{2,1,0:T(8,128)(2,1)} %get-tuple-element.1199), channel_id=1, source_target_pairs={{0,192},{64,0},{128,64},{192,128},{1,193},{65,1},{129,65},{193,129... | collective-permute-start | bytes 1572872 | tf_op jit(solution)/shard_map/while/body/eval_jaxpr/ppermute | solution.py:11
  240.7 6.1 copy-start.1
  261.3 7.0 collective-permute-start.1
  269.2 29.8 %collective-permute-start.2 = (bf16[2,128,1024]{2,1,0:T(8,128)(2,1)}, bf16[2,128,1024]{2,1,0:T(8,128)(2,1)S(1)}, u32[]{:S(2)}, u32[]{:S(2)}) collective-permute-start(bf16[2,128,1024]{2,1,0:T(8,128)(2,1)} %get-tuple-element.1212), channel_id=1, source_target_pairs={{0,192},{64,0},{128,64},{192,128},{1,193},{65,1},{129,65},{193,129... | collective-permute-start | bytes 1572872 | tf_op jit(solution)/shard_map/while/body/eval_jaxpr/ppermute | solution.py:11
  300.0 13.0 %collective-permute-start.2 = (bf16[2,128,1024]{2,1,0:T(8,128)(2,1)}, bf16[2,128,1024]{2,1,0:T(8,128)(2,1)S(1)}, u32[]{:S(2)}, u32[]{:S(2)}) collective-permute-start(bf16[2,128,1024]{2,1,0:T(8,128)(2,1)} %get-tuple-element.1212), channel_id=1, source_target_pairs={{0,192},{64,0},{128,64},{192,128},{1,193},{65,1},{129,65},{193,129... | collective-permute-start | bytes 1572872 | tf_op jit(solution)/shard_map/while/body/eval_jaxpr/ppermute | solution.py:11
  313.0 6.1 copy-start.2
  333.4 10.4 %collective-permute-start.2 = (bf16[2,128,1024]{2,1,0:T(8,128)(2,1)}, bf16[2,128,1024]{2,1,0:T(8,128)(2,1)S(1)}, u32[]{:S(2)}, u32[]{:S(2)}) collective-permute-start(bf16[2,128,1024]{2,1,0:T(8,128)(2,1)} %get-tuple-element.1212), channel_id=1, source_target_pairs={{0,192},{64,0},{128,64},{192,128},{1,193},{65,1},{129,65},{193,129... | collective-permute-start | bytes 1572872 | tf_op jit(solution)/shard_map/while/body/eval_jaxpr/ppermute | solution.py:11
  343.8 6.1 copy-start.2
  364.2 7.0 collective-permute-start.2
  372.3 647.0 %reduce-scatter.5.cloned.1.call-start = ((), (), s32[]{:S(2)}) async-start(), calls=%async_computation.2 | async-start | bytes 8519680 | tf_op jit(solution)/shard_map/reduce_scatter | solution.py:154
Sparse Core Ops, SparseCore 0:
  372.4 317.4 reduce-scatter.6
  692.6 326.6 reduce-scatter.4
where the time goes:
time: 1030 us
  waiting for transfers between devices  819 us (80%)
  starting transfers between devices  72.2 us (7%)
  matrix products  65.4 us (6%)
  other arithmetic  43 us (4%)
  between operations  14.1 us (1%)
  local copies, waits for them, and re-layouts  13.2 us (1%)
    reduce_scatter x1, waiting for transfers between devices, on_device(): lax.psum_scatter(grad_w, 'dp', scatter_dimension=1, tiled=True)  328 us
    unnamed x3, waiting for transfers between devices  318 us
    ppermute x18, waiting for transfers between devices, from_behind(): lax.ppermute(x, axis, [(i, (i + by) % length) for i in range(length)])  173 us
    ppermute x18, starting transfers between devices, from_behind(): lax.ppermute(x, axis, [(i, (i + by) % length) for i in range(length)])  72.1 us
    dot_general x8, matrix products, backward_section(): lax.dot_general(section_in[instant], grad_round, (((0,), (0,)), ((), ()))...  25.5 us
  transfers between devices with their start and end apart: 20, of which 20 were waited for; matrix products, arithmetic and copies ran while one was open for 0% of the time, Pallas kernels for 0%

commit v1 on v0

v1 whole, which is shorter than its diff:
```python
import functools

import jax
import jax.numpy as jnp
from jax import lax
from jax.experimental import pallas as pl
from jax.experimental.pallas import tpu as pltpu
from jax.sharding import PartitionSpec as P

MESH = pl.DeviceIdType.MESH
F32 = jnp.float32
BF16 = jnp.bfloat16
C = 1024
ROWS = 256
HALF = 128
NY, NZ = 4, 8
GAIN = 4.0

STREAMS = (
    (0, 384, 256, ("y", "z", "x")),
    (384, 384, 128, ("z", "y", "x")),
    (768, 256, 128, ("x", "y", "z")),
)
SIZES = {"x": 2, "y": NY, "z": NZ}


def stage_plan():
    plan = {}
    for r in range(2):
        for s, (_, width, left, order) in enumerate(STREAMS):
            span = {"x": 2, "y": NY, "z": NZ}
            for axis in order:
                span[axis] = 1
                shape = (span["x"], span["y"], span["z"], 16)
                if axis == "x":
                    plan[(r, s, axis, 0, 1)] = shape + (width,)
                else:
                    for hop in range(1, SIZES[axis] // 2 + 1):
                        plan[(r, s, axis, 0, hop)] = shape + (left if hop == 1 else width,)
                        plan[(r, s, axis, 1, hop)] = shape + (width - left if hop == 1 else width,)
    return plan


PLAN = stage_plan()
KEYS = list(PLAN)


def kernel(currents, weights, decay, out_grad, gw_ref, gd_ref, *scratch):
    (w, act, kept, gq, g, p_act, p_gq, part, dec, dd, dd_in, dv, dy, dz, dx) = scratch[:15]
    (l_sem, dec_sem, cw_s, cw_r, xh_s, pc_r, gs, half_r, pa_s, pa_r, pg_s, pg_r, dd_s, dd_r, dv_s, dv_r, rs_s, rs_r) = scratch[15:33]
    landing = dict(zip(KEYS, scratch[33:]))
    number = {key: i for i, key in enumerate(KEYS)}

    sec = lax.axis_index("section")
    dp = lax.axis_index("dp")
    xh, c = sec // 2, sec % 2
    xl, y, z = dp // 32, (dp // 8) % 4, dp % 8

    def device(xh=xh, c=c, xl=xl, y=y, z=z):
        return (xh * 2 + c, xl * 32 + y * 8 + z)

    core = device(c=1 - c)
    to_xl = device(xl=1 - xl)
    y_by = lambda k: device(y=(y + k) % NY)
    z_by = lambda k: device(z=(z + k) % NZ)
    across = lambda core_there: device(xh=1 - xh, xl=1 - xl, c=core_there)

    def remote(src, dst, send, recv, to):
        return pltpu.make_async_remote_copy(
            src_ref=src, dst_ref=dst, send_sem=send, recv_sem=recv, device_id=to, device_id_type=MESH
        )

    local = []
    for r in range(2):
        local.append(pltpu.make_async_copy(weights.at[r], w.at[r * 4 + sec], l_sem.at[r]))
    local.append(pltpu.make_async_copy(currents.at[c], act.at[0], l_sem.at[2]))
    local.append(pltpu.make_async_copy(out_grad.at[c], g, l_sem.at[3]))
    local.append(pltpu.make_async_copy(decay, dec.at[sec], l_sem.at[4]))
    for copy in local:
        copy.start()

    partners = [core, to_xl, across(c), across(1 - c)]
    partners += [y_by(k) for k in range(1, NY)] + [z_by(k) for k in range(1, NZ)]
    barrier = pltpu.get_barrier_semaphore()
    for partner in partners:
        pl.semaphore_signal(barrier, inc=1, device_id=partner, device_id_type=MESH)
    pl.semaphore_wait(barrier, len(partners))

    colour_there = (4 * (1 - xl) + 2 * y + z) % 8
    colour = (4 * xl + 2 * y + z) % 8

    def rows_of(half, unit, low, count):
        start = half * 512 + (unit % 8) * 64 + low
        return pl.ds(pl.multiple_of(start, 32), count)

    dec_copies = []
    for i, to in enumerate((core, across(c), across(1 - c))):
        dec_copies.append(remote(decay, dec.at[sec], dec_sem.at[0, i], dec_sem.at[1, i], to))
    for copy in dec_copies:
        copy.start()
    for r in range(2):
        layer = r * 4 + sec
        for half in range(2):
            for piece, (unit, low, count) in enumerate(((0, 0, 64), (3, 0, 32))):
                rows = rows_of(half, colour_there + unit, low, count)
                remote(
                    weights.at[r, rows], w.at[layer, rows], xh_s, pc_r.at[r * 2 + c, piece], across(half)
                ).start()
        remote(weights.at[r], w.at[layer], cw_s.at[r], cw_r.at[r], core).start()

    def layer_of(q):
        return (q // 2) * 4 + (1 - xh) * 2 + q % 2

    UNITS = ((0, 0, 64), (3, 0, 32), (1, 0, 64), (7, 0, 64), (2, 0, 64), (6, 0, 64), (4, 0, 64), (3, 32, 32), (5, 0, 32), (5, 32, 32))

    def pass_on(q, unit, low, count, piece, to):
        rows = rows_of(c, colour + unit, low, count)
        here = w.at[layer_of(q), rows]
        recv = half_r.at[q] if piece is None else pc_r.at[q, piece]
        remote(here, here, gs.at[q], recv, to).start()

    def arrived(q, piece):
        unit, low, count = UNITS[piece]
        here = w.at[layer_of(q), rows_of(c, colour + unit, low, count)]
        pltpu.make_async_copy(here, here, pc_r.at[q, piece]).wait()
        pass_on(q, unit, low, count, None, core)

    def first_hop(q):
        arrived(q, 0)
        for piece, to in ((3, z_by(1)), (2, z_by(7)), (5, y_by(1)), (4, y_by(3)), (6, to_xl)):
            pass_on(q, 0, 0, 64, piece, to)

    def second_hop(q):
        arrived(q, 2)
        pass_on(q, 1, 32, 32, 7, y_by(3))
        pass_on(q, 1, 32, 32, 9, to_xl)
        arrived(q, 3)
        pass_on(q, 7, 0, 32, 8, y_by(1))

    def rest(q):
        for piece in (1, 4, 5, 6, 7, 8, 9):
            arrived(q, piece)

    def tile(j, size=256):
        return pl.ds(pl.multiple_of(j * size, size), size)

    def own_chip(layer):
        return (layer // 2) % 2 == xh

    def forward(layer):
        lap = layer // 4

        @pl.when(own_chip(layer) & (layer % 2 == c))
        def _():
            pltpu.make_async_copy(weights.at[lap], w.at[layer], l_sem.at[lap]).wait()

        @pl.when(own_chip(layer) & (layer % 2 != c))
        def _():
            pltpu.make_async_copy(w.at[layer], w.at[layer], cw_r.at[lap]).wait()
            remote(act.at[layer], p_act.at[lap], pa_s.at[lap], pa_r.at[lap], core).start()

        @pl.when(jnp.logical_not(own_chip(layer)))
        def _():
            half = w.at[layer, pl.ds(pl.multiple_of((1 - c) * 512, 512), 512)]
            pltpu.make_async_copy(half, half, half_r.at[lap * 2 + layer % 2]).wait()

        @pl.loop(0, 4)
        def _(j):
            cols = tile(j)
            pre = jnp.dot(act[layer], w[layer, :, cols], preferred_element_type=F32)
            rate = dec[layer % 4, lap, :, cols]
            old = act[layer, :, cols].astype(F32)
            h0 = pre[:HALF]
            s0 = 1.0 / (1.0 + jnp.exp(-GAIN * (h0 - 1.0)))
            rest0 = 1.0 - s0
            v0 = h0 * rest0
            h1 = rate * v0 + pre[HALF:]
            s1 = 1.0 / (1.0 + jnp.exp(-GAIN * (h1 - 1.0)))
            slope0 = GAIN * s0 * rest0
            kept[layer, 0, :, cols] = slope0
            kept[layer, 1, :, cols] = GAIN * s1 * (1.0 - s1)
            kept[layer, 2, :, cols] = rate * (rest0 - h0 * slope0)
            kept[layer, 3, :, cols] = v0
            act[layer + 1, pl.ds(0, HALF), cols] = (old[:HALF] + s0).astype(BF16)
            act[layer + 1, pl.ds(HALF, HALF), cols] = (old[HALF:] + s1).astype(BF16)

    def backward(layer, with_input=True):
        lap = layer // 4

        @pl.loop(0, 4)
        def _(j):
            cols = tile(j)
            gh1 = g[pl.ds(HALF, HALF), cols].astype(F32) * kept[layer, 1, :, cols]
            gh0 = g[pl.ds(0, HALF), cols].astype(F32) * kept[layer, 0, :, cols] + gh1 * kept[layer, 2, :, cols]
            gq[layer, pl.ds(0, HALF), cols] = gh0.astype(BF16)
            gq[layer, pl.ds(HALF, HALF), cols] = gh1.astype(BF16)
            dd[layer, :, cols] = jnp.sum(gh1 * kept[layer, 3, :, cols], axis=0, keepdims=True)

        @pl.when(own_chip(layer) & (layer % 2 != c))
        def _():
            remote(gq.at[layer], p_gq.at[lap], pg_s.at[lap], pg_r.at[lap], core).start()
            remote(dd.at[layer], dd_in.at[lap], dd_s.at[lap], dd_r.at[lap], core).start()

        if with_input:

            @pl.loop(0, 4)
            def _(j):
                cols = tile(j)
                back = lax.dot_general(
                    gq[layer], w[layer, cols, :], (((1,), (1,)), ((), ())), preferred_element_type=F32
                )
                g[:, cols] = (g[:, cols].astype(F32) + back).astype(BF16)

    def weight_gradient(lap):
        layer = lap * 4 + sec
        pltpu.make_async_copy(p_act.at[lap], p_act.at[lap], pa_r.at[lap]).wait()
        pltpu.make_async_copy(p_gq.at[lap], p_gq.at[lap], pg_r.at[lap]).wait()
        pltpu.make_async_copy(dd_in.at[lap], dd_in.at[lap], dd_r.at[lap]).wait()
        dv[pl.ds(lap, 1), :] = dd[layer] + dd_in[lap]
        over_rows = (((0,), (0,)), ((), ()))

        @pl.loop(0, 4)
        def _(i):
            for n in range(2):
                cols = pl.ds(n * 512, 512)
                total = lax.dot_general(
                    act[layer, :, tile(i)], gq[layer, :, cols], over_rows, preferred_element_type=F32
                ) + lax.dot_general(
                    p_act[lap, :, tile(i)], p_gq[lap, :, cols], over_rows, preferred_element_type=F32
                )
                part[lap, i // 2, pl.ds((i % 2) * 2, 2), :, :, cols] = total.astype(BF16).reshape(2, 8, 16, 512)

    sums = []

    def stream(r, s):
        first, width, left, order = STREAMS[s]
        where = {"x": pl.ds(0, 2), "y": pl.ds(0, NY), "z": pl.ds(0, NZ)}
        mine = {"x": xl, "y": y, "z": z}

        def chunk(axis, place, low=0, count=width):
            at = dict(where)
            at[axis] = pl.ds(place, 1)
            return part.at[r, at["x"], at["y"], at["z"], :, pl.ds(first + low, count)]

        def send(src, key, to):
            i = number[key]
            copy = remote(src, landing[key], rs_s.at[i], rs_r.at[i], to)
            copy.start()
            sums.append(copy)

        def wait(key):
            i = number[key]
            pltpu.make_async_copy(landing[key], landing[key], rs_r.at[i]).wait()

        for axis in order:
            last = axis == order[-1]
            n = SIZES[axis]
            me = mine[axis]
            if axis == "x":
                key = (r, s, axis, 0, 1)
                send(chunk(axis, 1 - me), key, to_xl)
                yield
                wait(key)
                terms = [landing[key][...]]
            else:
                by = y_by if axis == "y" else z_by
                far = n // 2
                send(chunk(axis, (me + far) % n, 0, left), (r, s, axis, 0, 1), by(1))
                send(chunk(axis, (me + far) % n, left, width - left), (r, s, axis, 1, 1), by(n - 1))
                yield
                for hop in range(2, far + 1):
                    for way in range(2):
                        step = far - hop + 1
                        place = (me + (step if way == 0 else n - step)) % n
                        came = (r, s, axis, way, hop - 1)
                        wait(came)
                        low, count = (0, width) if hop > 2 else ((0, left) if way == 0 else (left, width - left))
                        here = chunk(axis, place, low, count)
                        here[...] = (here[...].astype(F32) + landing[came][...].astype(F32)).astype(BF16)
                        send(chunk(axis, place), (r, s, axis, way, hop), by(1 if way == 0 else n - 1))
                    yield
                for way in range(2):
                    wait((r, s, axis, way, far))
                terms = [landing[(r, s, axis, way, far)][...] for way in range(2)]
            own = chunk(axis, me)
            total = own[...].astype(F32)
            for term in terms:
                total = total + term.astype(F32)
            where[axis] = pl.ds(me, 1)
            if last:
                gw_ref[r, :, pl.ds(first, width)] = total.astype(BF16).reshape(16, width)
            else:
                own[...] = total.astype(BF16)

    def advance(streams):
        going = []
        for one in streams:
            try:
                next(one)
                going.append(one)
            except StopIteration:
                pass
        return going

    start = 2 - 2 * xh
    local[2].wait()
    local[4].wait()
    for copy in dec_copies:
        copy.wait_recv()

    def forward_loop(low, high):
        def body(layer, carry):
            forward(layer)
            return carry

        lax.fori_loop(low, high, body, 0)

    forward_loop(0, start)
    for q in (0, 1):
        first_hop(q)
    for q in (0, 1):
        second_hop(q)
    for q in (0, 1):
        rest(q)
    forward(start)
    first_hop(2)
    forward(start + 1)
    first_hop(3)
    second_hop(2)
    forward(start + 2)
    second_hop(3)
    forward(start + 3)
    rest(2)
    rest(3)
    forward_loop(start + 4, 8)

    local[3].wait()
    count = 4 - 2 * xh

    def body(i, carry):
        backward(7 - i)
        return carry

    lax.fori_loop(0, count, body, 0)
    weight_gradient(1)
    streams = advance([stream(1, s) for s in range(len(STREAMS))])
    for i in range(4):
        backward(7 - count - i, with_input=i < 3)
        streams = advance(streams)
    weight_gradient(0)
    streams = streams + [stream(0, s) for s in range(len(STREAMS))]
    streams = advance(streams[-len(STREAMS):]) + streams[: -len(STREAMS)]

    decay_copies = []

    def swap(buffer, by, n, base):
        copies = []
        for k in range(1, n):
            copies.append(remote(dv, buffer.at[k - 1], dv_s.at[base + k], dv_r.at[base + k], by(k)))
            copies[-1].start()
        return copies

    def gather_in(copies, buffer):
        for copy in copies:
            copy.wait()
        total = dv[...]
        for k in range(len(copies)):
            total = total + buffer[k]
        dv[...] = total

    copies = swap(dy, y_by, NY, 0)
    streams = advance(streams)
    gather_in(copies, dy)
    copies = swap(dz, z_by, NZ, 8)
    streams = advance(streams)
    streams = advance(streams)
    gather_in(copies, dz)
    copies = swap(dx, lambda k: to_xl, 2, 20)
    streams = advance(streams)
    gather_in(copies, dx)
    gd_ref[...] = pltpu.roll(dv[...], (C - dp * 16) % C, axis=1)[:, :16]
    while streams:
        streams = advance(streams)

    for copy in sums:
        copy.wait_send()
    for copy in dec_copies:
        copy.wait_send()
    sent = w.at[0, pl.ds(0, 384)]
    pltpu.make_async_copy(sent, sent, xh_s).wait()
    for q in range(4):
        sent = w.at[0, pl.ds(0, 928)]
        pltpu.make_async_copy(sent, sent, gs.at[q]).wait()
    for r in range(2):
        pltpu.make_async_copy(w.at[0], w.at[0], cw_s.at[r]).wait()
        pltpu.make_async_copy(p_act.at[r], p_act.at[r], pa_s.at[r]).wait()
        pltpu.make_async_copy(p_gq.at[r], p_gq.at[r], pg_s.at[r]).wait()
        pltpu.make_async_copy(dd_in.at[r], dd_in.at[r], dd_s.at[r]).wait()


def on_device(currents, weights, decay, out_grad):
    dma = pltpu.SemaphoreType.DMA
    vmem = pltpu.VMEM
    scratch = [
        vmem((8, C, C), BF16),
        vmem((9, ROWS, C), BF16),
        vmem((8, 4, HALF, C), F32),
        vmem((8, ROWS, C), BF16),
        vmem((ROWS, C), BF16),
        vmem((2, ROWS, C), BF16),
        vmem((2, ROWS, C), BF16),
        vmem((2, 2, NY, NZ, 16, C), BF16),
        vmem((4, 2, 1, C), F32),
        vmem((8, 1, C), F32),
        vmem((2, 1, C), F32),
        vmem((2, C), F32),
        vmem((NY - 1, 2, C), F32),
        vmem((NZ - 1, 2, C), F32),
        vmem((1, 2, C), F32),
        dma((5,)), dma((2, 3)), dma((2,)), dma((2,)), dma, dma((4, 10)), dma((4,)), dma((4,)),
        dma((2,)), dma((2,)), dma((2,)), dma((2,)), dma((2,)), dma((2,)), dma((24,)), dma((24,)),
        dma((len(KEYS),)), dma((len(KEYS),)),
    ] + [vmem(PLAN[key], BF16) for key in KEYS]
    anywhere = pl.BlockSpec(memory_space=pl.ANY)
    in_vmem = pl.BlockSpec(memory_space=pltpu.VMEM)
    gw, gd = pl.pallas_call(
        kernel,
        out_shape=(jax.ShapeDtypeStruct((2, 16, C), BF16), jax.ShapeDtypeStruct((2, 16), F32)),
        in_specs=[anywhere] * 4,
        out_specs=(in_vmem, in_vmem),
        scratch_shapes=scratch,
        compiler_params=pltpu.CompilerParams(
            collective_id=0, has_side_effects=True, vmem_limit_bytes=60 * 2**20
        ),
        name="relay",
    )(
        currents.reshape(2, ROWS, C),
        weights.reshape(2, C, C),
        decay,
        out_grad.reshape(2, ROWS, C),
    )
    return gw[:, None], gd[:, None]


def solution(mesh):
    in_specs = (
        P(None, None, "dp", None),
        P(None, "section", None, None),
        P(None, "section", None),
        P(None, None, "dp", None),
    )
    out_specs = (P(None, "section", "dp", None), P(None, "section", "dp"))
    return jax.shard_map(on_device, mesh=mesh, in_specs=in_specs, out_specs=out_specs, check_vma=False)
```

time: 1030 us -> 112 us (0.11)
  waiting for transfers between devices: 819 us -> 0 us
  Pallas kernels: 0 us -> 107 us
  starting transfers between devices: 72.2 us -> 0 us
  matrix products: 65.4 us -> 0 us
  other arithmetic: 43 us -> 0 us
  between operations: 14.1 us -> 0.64 us
  local copies, waits for them, and re-layouts: 13.2 us -> 2.67 us
    reduce_scatter x1 -> x0, waiting for transfers between devices: 328 us -> none  [on_device(): lax.psum_scatter(grad_w, 'dp', scatter_dimension=1, tiled=True)]
    unnamed x3 -> x0, waiting for transfers between devices: 318 us -> none
    ppermute x18 -> x0, waiting for transfers between devices: 173 us -> none  [from_behind(): lax.ppermute(x, axis, [(i, (i + by) % length) for i in range(length)])]
    pallas_call x0 -> x1, Pallas kernels: none -> 107 us  [on_device(): pl.pallas_call(kernel, out_shape=(jax.ShapeDtypeStruct((2, 16, C), BF16),...]
    ppermute x18 -> x0, starting transfers between devices: 72.1 us -> none  [from_behind(): lax.ppermute(x, axis, [(i, (i + by) % length) for i in range(length)])]
    dot_general x32 -> x0, matrix products: 65.4 us -> none  [the longest x8 25.5 us: backward_section(): lax.dot_general(section_in[instant], grad_round, (((0,), (0,)), ((), ()))...]
    another operation x20 -> x0, other arithmetic: 23.7 us -> none
  transfers between devices with their start and end apart: 20 -> 0, of which waited for: 20 -> 0; matrix products, arithmetic and copies ran while one was open for 0% -> 0% of each run, Pallas kernels for 0% -> 0%
where the time goes in v1:
time: 112 us; the launch traced here: 111 us
  Pallas kernels  107 us (96%)
  local copies, waits for them, and re-layouts  2.67 us (2%)
    pallas_call x1, Pallas kernels, on_device(): pl.pallas_call(kernel, out_shape=(jax.ShapeDtypeStruct((2, 16, C), BF16),...  107 us
    unnamed x2, local copies, waits for them, and re-layouts  2.67 us

profile of v1, /device:TPU:2, one launch (start us, length us, event | category | flops | bytes accessed | tf_op | source)
XLA Modules:
  0.0 110.6 jit_solution(7675037944086859219)
XLA Ops:
  0.6 107.3 %relay.1 = (bf16[2,16,1024]{2,1,0:T(8,128)(2,1)}, f32[2,16]{1,0:T(2,128)}) custom-call(bf16[2,256,1024]{2,1,0:T(8,128)(2,1)} %bitcast.10, bf16[2,1024,1024]{2,1,0:T(8,128)(2,1)} %bitcast.9, f32[2,1,1024]{2,1,0:T(1,128)} %decay.1, bf16[2,256,1024]{2,1,0:T(8,128)(2,1)} %bitcast.11), custom_call_target="tpu_custom_call" | custom-call | tf_op jit(solution)/shard_map/relay/pallas_call | solution.py:426
  108.0 1.5 %copy.10 = bf16[2,1,16,1024]{3,2,1,0:T(8,128)(2,1)} copy(bf16[2,1,16,1024]{3,2,1,0:T(8,128)(2,1)} %bitcast.12) | data formatting | bytes 131072
  109.4 1.2 %copy.11 = f32[2,1,16]{2,1,0:T(1,128)} copy(f32[2,1,16]{2,1,0:T(1,128)} %bitcast.13) | data formatting | bytes 256

commit v2 on v1

v2 whole, which is shorter than its diff:
```python
import functools
import itertools

import jax
import jax.numpy as jnp
from jax import lax
from jax.experimental import pallas as pl
from jax.experimental.pallas import tpu as pltpu
from jax.sharding import PartitionSpec as P

MESH = pl.DeviceIdType.MESH
F32 = jnp.float32
BF16 = jnp.bfloat16
C = 1024
ROWS = 256
HALF = 128
NY, NZ = 4, 8
GAIN = 4.0

SUBS = 2
WINDOW = 1
UNIT = 64 // SUBS
X, Y, Z, ZD, YD, XYD = "x", "y", "z", "zd", "yd", "xyd"

STREAMS = (
    (
        (0, 2, (Z, Y, X,), -1),
        (2, 2, (X, Y, ZD,), -1),
        (4, 2, (Z, XYD,), -1),
        (6, 1, (Y, Z, X,), 1),
        (7, 1, (X, Y, ZD,), -1),
    ),
    (
        (0, 2, (X, Y, Z,), 1),
        (2, 2, (Z, YD, X,), 1),
        (4, 2, (Y, Z, X,), -1),
        (6, 2, (Y, Z, X,), 1),
    ),
)
ORDER = (
    16, 17, -1, 18, 19, -1, -1, -1, 17, 17, -1, -1, -2, 0, 18, 1, -1, 3, 2, 17,
    16, 19, 0, 0, 4, 17, 3, -2, 2, 2, 18, 16, 0, 17, 0, 1, 19, 2, 18, 18,
    3, 2, 4, -2, 0, 16, 1, 19, 19, 17, 3, 3, 18, 18, 2, 4, 16, 19, 0, 3,
    16, 3, 19, 18, 1, 16, 19, 3, 0, -2, 16, 2, 4, 16, 0, 17, 3, 18, 19, 1,
    0, 16, 2, 3, 17, 18, 19, 4,
)
SIZES = {"x": 2, "y": NY, "z": NZ}


def offsets(stage):
    return [o for o in itertools.product(*[range(SIZES[axis]) for axis in stage.rstrip("d")]) if any(o)]


def hops_of(axis, way):
    far = SIZES[axis] // 2
    return {way: far, -way: far - 1}


def landing_plan():
    plan = {}
    for r in range(2):
        for s, (_, blocks, order, way) in enumerate(STREAMS[r]):
            span = dict(SIZES)
            for stage in order:
                for axis in stage.rstrip("d"):
                    span[axis] = 1
                shape = (blocks, span["x"], span["y"], span["z"], 16, 128)
                if stage in ("y", "z"):
                    for d, count in hops_of(stage, way).items():
                        for hop in range(1, count + 1):
                            plan[(r, s, stage, d, hop)] = shape
                else:
                    for offset in offsets(stage):
                        plan[(r, s, stage, offset)] = shape
    return plan


PLAN = landing_plan()
KEYS = list(PLAN)


def kernel(currents, weights, decay, out_grad, gw_ref, gd_ref, *scratch):
    (w, act, kept, gq, g, p_act, p_gq, part, dec, dd, dd_in, dv, dy, dz, dx) = scratch[:15]
    (l_sem, dec_sem, cw_s, cw_r, xh_s, pc_r, gs, half_r, pa_s, pa_r, pg_s, pg_r, dd_s, dd_r, dv_s, dv_r, rs_s, rs_r) = scratch[15:33]
    landing = dict(zip(KEYS, scratch[33:]))
    number = {key: i for i, key in enumerate(KEYS)}

    sec = lax.axis_index("section")
    dp = lax.axis_index("dp")
    xh, c = sec // 2, sec % 2
    xl, y, z = dp // 32, (dp // 8) % 4, dp % 8

    def device(xh=xh, c=c, xl=xl, y=y, z=z):
        return (xh * 2 + c, xl * 32 + y * 8 + z)

    core = device(c=1 - c)
    to_xl = device(xl=1 - xl)
    y_by = lambda k: device(y=(y + k) % NY)
    z_by = lambda k: device(z=(z + k) % NZ)
    across = lambda core_there: device(xh=1 - xh, xl=1 - xl, c=core_there)

    def remote(src, dst, send, recv, to):
        return pltpu.make_async_remote_copy(
            src_ref=src, dst_ref=dst, send_sem=send, recv_sem=recv, device_id=to, device_id_type=MESH
        )

    local = []
    for r in range(2):
        local.append(pltpu.make_async_copy(weights.at[r], w.at[r * 4 + sec], l_sem.at[r]))
    local.append(pltpu.make_async_copy(currents.at[c], act.at[0], l_sem.at[2]))
    local.append(pltpu.make_async_copy(out_grad.at[c], g, l_sem.at[3]))
    local.append(pltpu.make_async_copy(decay, dec.at[sec], l_sem.at[4]))
    for copy in local:
        copy.start()

    partners = [core, to_xl, across(c), across(1 - c)]
    partners += [y_by(k) for k in range(1, NY)] + [z_by(k) for k in range(1, NZ)]
    partners += [device(xl=1 - xl, y=(y + k) % NY) for k in range(1, NY)]
    barrier = pltpu.get_barrier_semaphore()
    for partner in partners:
        pl.semaphore_signal(barrier, inc=1, device_id=partner, device_id_type=MESH)
    pl.semaphore_wait(barrier, len(partners))

    colour_there = (4 * (1 - xl) + 2 * y + z) % 8
    colour = (4 * xl + 2 * y + z) % 8

    def rows_of(half, sub, unit, low, count):
        start = half * 512 + sub * (512 // SUBS) + (unit % 8) * UNIT + low
        return pl.ds(pl.multiple_of(start, 16), count)

    dec_copies = []
    for i, to in enumerate((core, across(c), across(1 - c))):
        dec_copies.append(remote(decay, dec.at[sec], dec_sem.at[0, i], dec_sem.at[1, i], to))
    for copy in dec_copies:
        copy.start()

    def send_across(phase):
        r, sub = divmod(phase, SUBS)
        for piece, (unit, count) in enumerate(((0, UNIT), (3, UNIT // 2))):
            for half in range(2):
                rows = rows_of(half, sub, colour_there + unit, 0, count)
                remote(
                    weights.at[r, rows], w.at[r * 4 + sec, rows], xh_s, pc_r.at[r * 2 + c, sub, piece], across(half)
                ).start()

    for phase in range(WINDOW):
        send_across(phase)
    remote(weights.at[0], w.at[sec], cw_s.at[0], cw_r.at[0], core).start()

    def layer_of(q):
        return (q // 2) * 4 + (1 - xh) * 2 + q % 2

    low_half, high_half = (0, UNIT // 2), (UNIT // 2, UNIT // 2)
    every = (0, UNIT)
    PIECES = (
        (0, *every), (3, *low_half), (1, *every), (7, *every), (2, *every), (6, *every), (4, *every),
        (3, *high_half), (5, *low_half), (5, *high_half),
    )

    def pass_on(q, sub, unit, low, count, piece, to):
        here = w.at[layer_of(q), rows_of(c, sub, colour + unit, low, count)]
        remote(here, here, gs.at[q], pc_r.at[q, sub, piece], to).start()

    def arrived(q, sub, piece):
        unit, low, count = PIECES[piece]
        here = w.at[layer_of(q), rows_of(c, sub, colour + unit, low, count)]
        pltpu.make_async_copy(here, here, pc_r.at[q, sub, piece]).wait()

    def both(phase):
        lap, sub = divmod(phase, SUBS)
        return ((lap * 2, sub), (lap * 2 + 1, sub))

    def first_hop(phase):
        for q, sub in both(phase):
            arrived(q, sub, 0)
            for piece, to in ((4, y_by(3)), (5, y_by(1)), (6, to_xl), (3, z_by(1)), (2, z_by(7))):
                pass_on(q, sub, 0, *every, piece, to)
        if phase + WINDOW < 2 * SUBS:
            send_across(phase + WINDOW)
        if phase == SUBS - 1:
            remote(weights.at[1], w.at[4 + sec], cw_s.at[1], cw_r.at[1], core).start()

    def second_hop(phase):
        for q, sub in both(phase):
            arrived(q, sub, 2)
            pass_on(q, sub, 1, *high_half, 7, y_by(3))
            pass_on(q, sub, 1, *high_half, 9, to_xl)
            arrived(q, sub, 3)
            pass_on(q, sub, 7, *low_half, 8, y_by(1))

    def rest(phase):
        for q, sub in both(phase):
            for piece in (1, 4, 5, 6, 7, 8, 9):
                arrived(q, sub, piece)
            start = c * 512 + sub * (512 // SUBS)
            here = w.at[layer_of(q), pl.ds(pl.multiple_of(start, 128), 512 // SUBS)]
            remote(here, here, gs.at[q], half_r.at[q, sub], core).start()

    def tile(j, size=256):
        return pl.ds(pl.multiple_of(j * size, size), size)

    def own_chip(layer):
        return (layer // 2) % 2 == xh

    def forward(layer):
        lap = layer // 4

        @pl.when(own_chip(layer) & (layer % 2 == c))
        def _():
            pltpu.make_async_copy(weights.at[lap], w.at[layer], l_sem.at[lap]).wait()

        @pl.when(own_chip(layer) & (layer % 2 != c))
        def _():
            pltpu.make_async_copy(w.at[layer], w.at[layer], cw_r.at[lap]).wait()
            remote(act.at[layer], p_act.at[lap], pa_s.at[lap], pa_r.at[lap], core).start()

        @pl.when(jnp.logical_not(own_chip(layer)))
        def _():
            for sub in range(SUBS):
                start = (1 - c) * 512 + sub * (512 // SUBS)
                here = w.at[layer, pl.ds(pl.multiple_of(start, 128), 512 // SUBS)]
                pltpu.make_async_copy(here, here, half_r.at[lap * 2 + layer % 2, sub]).wait()

        @pl.loop(0, 4, unroll=True)
        def _(j):
            cols = tile(j)
            pre = jnp.dot(act[layer], w[layer, :, cols], preferred_element_type=F32)
            rate = dec[layer % 4, lap, :, cols]
            old = act[layer, :, cols].astype(F32)
            h0 = pre[:HALF]
            s0 = 1.0 / (1.0 + jnp.exp(-GAIN * (h0 - 1.0)))
            rest0 = 1.0 - s0
            v0 = h0 * rest0
            h1 = rate * v0 + pre[HALF:]
            s1 = 1.0 / (1.0 + jnp.exp(-GAIN * (h1 - 1.0)))
            slope0 = GAIN * s0 * rest0
            kept[layer, 0, :, cols] = slope0
            kept[layer, 1, :, cols] = GAIN * s1 * (1.0 - s1)
            kept[layer, 2, :, cols] = rate * (rest0 - h0 * slope0)
            kept[layer, 3, :, cols] = v0
            act[layer + 1, pl.ds(0, HALF), cols] = (old[:HALF] + s0).astype(BF16)
            act[layer + 1, pl.ds(HALF, HALF), cols] = (old[HALF:] + s1).astype(BF16)

    def backward(layer, with_input=True):
        lap = layer // 4

        @pl.loop(0, 4, unroll=True)
        def _(j):
            cols = tile(j)
            gh1 = g[pl.ds(HALF, HALF), cols].astype(F32) * kept[layer, 1, :, cols]
            gh0 = g[pl.ds(0, HALF), cols].astype(F32) * kept[layer, 0, :, cols] + gh1 * kept[layer, 2, :, cols]
            gq[layer, pl.ds(0, HALF), cols] = gh0.astype(BF16)
            gq[layer, pl.ds(HALF, HALF), cols] = gh1.astype(BF16)
            dd[layer, :, cols] = jnp.sum(gh1 * kept[layer, 3, :, cols], axis=0, keepdims=True)

        @pl.when(own_chip(layer) & (layer % 2 != c))
        def _():
            remote(gq.at[layer], p_gq.at[lap], pg_s.at[lap], pg_r.at[lap], core).start()
            remote(dd.at[layer], dd_in.at[lap], dd_s.at[lap], dd_r.at[lap], core).start()

        if with_input:

            @pl.loop(0, 4, unroll=True)
            def _(j):
                cols = tile(j)
                back = lax.dot_general(
                    gq[layer], w[layer, cols, :], (((1,), (1,)), ((), ())), preferred_element_type=F32
                )
                g[:, cols] = (g[:, cols].astype(F32) + back).astype(BF16)

    def weight_gradient(lap, n):
        layer = lap * 4 + sec
        if n == 0:
            pltpu.make_async_copy(p_act.at[lap], p_act.at[lap], pa_r.at[lap]).wait()
            pltpu.make_async_copy(p_gq.at[lap], p_gq.at[lap], pg_r.at[lap]).wait()
            pltpu.make_async_copy(dd_in.at[lap], dd_in.at[lap], dd_r.at[lap]).wait()
            dv[pl.ds(lap, 1), :] = dd[layer] + dd_in[lap]
        over_rows = (((0,), (0,)), ((), ()))
        cols = pl.ds(n * 512, 512)

        @pl.loop(0, 4, unroll=True)
        def _(i):
            total = lax.dot_general(
                act[layer, :, tile(i)], gq[layer, :, cols], over_rows, preferred_element_type=F32
            ) + lax.dot_general(
                p_act[lap, :, tile(i)], p_gq[lap, :, cols], over_rows, preferred_element_type=F32
            )
            for b in range(4):
                block = total[:, b * 128 : (b + 1) * 128].astype(BF16).reshape(2, 8, 16, 128)
                part[lap, n * 4 + b, i // 2, pl.ds((i % 2) * 2, 2)] = block

    sums = []

    def stream(r, s):
        first, blocks, order, way = STREAMS[r][s]
        where = {"x": pl.ds(0, 2), "y": pl.ds(0, NY), "z": pl.ds(0, NZ)}
        mine = {"x": xl, "y": y, "z": z}

        def chunk(places):
            at = {**where, **{axis: pl.ds(place, 1) for axis, place in places.items()}}
            return part.at[r, pl.ds(first, blocks), at["x"], at["y"], at["z"]]

        def send(places, key, to):
            i = number[key]
            copy = remote(chunk(places), landing[key], rs_s.at[i], rs_r.at[i], to)
            copy.start()
            sums.append(copy)

        def wait(key):
            i = number[key]
            pltpu.make_async_copy(landing[key], landing[key], rs_r.at[i]).wait()

        def own_sum(keys):
            for key in keys:
                wait(key)
            total = chunk({})[...].astype(F32)
            for key in keys:
                total = total + landing[key][...].astype(F32)
            return total

        pending = []
        for stage in order:
            if pending:
                chunk({})[...] = own_sum(pending).astype(BF16)
            if stage in ("y", "z"):
                n, me = SIZES[stage], mine[stage]
                by = y_by if stage == "y" else z_by
                hops = hops_of(stage, way)
                for d in (1, -1):
                    send({stage: (me + d * hops[d] + n) % n}, (r, s, stage, d, 1), by((d + n) % n))
                yield
                for hop in range(2, n // 2 + 1):
                    for d in (way, -way):
                        if hop > hops[d]:
                            continue
                        to = {stage: (me + d * (hops[d] - hop + 1) + n) % n}
                        came = (r, s, stage, d, hop - 1)
                        wait(came)
                        here = chunk(to)
                        here[...] = (here[...].astype(F32) + landing[came][...].astype(F32)).astype(BF16)
                        send(to, (r, s, stage, d, hop), by((d + n) % n))
                        yield
                pending = [(r, s, stage, d, hops[d]) for d in (1, -1)]
                where[stage] = pl.ds(me, 1)
            else:
                axes = stage.rstrip("d")
                pending = []
                for offset in offsets(stage):
                    to = {axis: (mine[axis] + by) % SIZES[axis] for axis, by in zip(axes, offset)}
                    names = {"x": "xl", "y": "y", "z": "z"}
                    send(to, (r, s, stage, offset), device(**{names[axis]: place for axis, place in to.items()}))
                    pending.append((r, s, stage, offset))
                yield
                for axis in axes:
                    where[axis] = pl.ds(mine[axis], 1)
        total = own_sum(pending).astype(BF16)
        for b in range(blocks):
            gw_ref[r, :, pl.ds((first + b) * 128, 128)] = total[b, 0, 0, 0]

    def decay_sum():
        for i, (buffer, by, n) in enumerate(((dy, y_by, NY), (dz, z_by, NZ), (dx, lambda k: to_xl, 2))):
            copies = []
            for k in range(1, n):
                copies.append(remote(dv, buffer.at[k - 1], dv_s.at[i * 8 + k], dv_r.at[i * 8 + k], by(k)))
                copies[-1].start()
            yield
            for copy in copies:
                copy.wait()
            total = dv[...]
            for k in range(n - 1):
                total = total + buffer[k]
            dv[...] = total
        gd_ref[...] = pltpu.roll(dv[...], (C - dp * 16) % C, axis=1)[:, :16]

    start = 2 - 2 * xh
    local[2].wait()
    local[4].wait()
    for copy in dec_copies:
        copy.wait_recv()

    def forward_loop(low, high):
        def body(layer, carry):
            forward(layer)
            return carry

        lax.fori_loop(low, high, body, 0)

    forward_loop(0, start)
    done = 0
    for step in range(2 * SUBS + 2):
        if step < 2 * SUBS:
            first_hop(step)
        if 0 <= step - 1 < 2 * SUBS:
            second_hop(step - 1)
        if step - 2 >= 0:
            rest(step - 2)
        if SUBS + 1 <= step < 2 * SUBS + 1 and done < 4:
            forward(start + done)
            done += 1
    forward_loop(start + done, 8)

    local[3].wait()
    count = 4 - 2 * xh

    def body(i, carry):
        backward(7 - i)
        return carry

    lax.fori_loop(0, count, body, 0)
    weight_gradient(1, 0)
    pieces = [functools.partial(weight_gradient, 1, 1)]
    pieces += [functools.partial(backward, 7 - count - i, i < 3) for i in range(4)]
    pieces += [functools.partial(weight_gradient, 0, n) for n in range(2)]
    streams = {r * 16 + s: stream(r, s) for r in range(2) for s in range(len(STREAMS[r]))}
    streams[-2] = decay_sum()

    def advance(key):
        if key == -1:
            pieces.pop(0)()
        elif next(streams[key], 0) is not None:
            del streams[key]

    for key in ORDER:
        advance(key)
    assert not streams and not pieces

    for copy in sums:
        copy.wait_send()
    for copy in dec_copies:
        copy.wait_send()
    sent = w.at[0, pl.ds(0, 384)]
    pltpu.make_async_copy(sent, sent, xh_s).wait()
    for q in range(4):
        sent = w.at[0, pl.ds(0, 928)]
        pltpu.make_async_copy(sent, sent, gs.at[q]).wait()
    for r in range(2):
        pltpu.make_async_copy(w.at[0], w.at[0], cw_s.at[r]).wait()
        pltpu.make_async_copy(p_act.at[r], p_act.at[r], pa_s.at[r]).wait()
        pltpu.make_async_copy(p_gq.at[r], p_gq.at[r], pg_s.at[r]).wait()
        pltpu.make_async_copy(dd_in.at[r], dd_in.at[r], dd_s.at[r]).wait()


def on_device(currents, weights, decay, out_grad):
    dma = pltpu.SemaphoreType.DMA
    vmem = pltpu.VMEM
    scratch = [
        vmem((8, C, C), BF16),
        vmem((9, ROWS, C), BF16),
        vmem((8, 4, HALF, C), F32),
        vmem((8, ROWS, C), BF16),
        vmem((ROWS, C), BF16),
        vmem((2, ROWS, C), BF16),
        vmem((2, ROWS, C), BF16),
        vmem((2, 8, 2, NY, NZ, 16, 128), BF16),
        vmem((4, 2, 1, C), F32),
        vmem((8, 1, C), F32),
        vmem((2, 1, C), F32),
        vmem((2, C), F32),
        vmem((NY - 1, 2, C), F32),
        vmem((NZ - 1, 2, C), F32),
        vmem((1, 2, C), F32),
        dma((5,)), dma((2, 3)), dma((2,)), dma((2,)), dma, dma((4, SUBS, 10)), dma((4,)), dma((4, SUBS)),
        dma((2,)), dma((2,)), dma((2,)), dma((2,)), dma((2,)), dma((2,)), dma((24,)), dma((24,)),
        dma((len(KEYS),)), dma((len(KEYS),)),
    ] + [vmem(PLAN[key], BF16) for key in KEYS]
    anywhere = pl.BlockSpec(memory_space=pl.ANY)
    in_vmem = pl.BlockSpec(memory_space=pltpu.VMEM)
    gw, gd = pl.pallas_call(
        kernel,
        out_shape=(jax.ShapeDtypeStruct((2, 16, C), BF16), jax.ShapeDtypeStruct((2, 16), F32)),
        in_specs=[anywhere] * 4,
        out_specs=(in_vmem, in_vmem),
        scratch_shapes=scratch,
        compiler_params=pltpu.CompilerParams(
            collective_id=0, has_side_effects=True, vmem_limit_bytes=60 * 2**20
        ),
        name="relay",
    )(
        currents.reshape(2, ROWS, C),
        weights.reshape(2, C, C),
        decay,
        out_grad.reshape(2, ROWS, C),
    )
    return gw[:, None], gd[:, None]


def solution(mesh):
    in_specs = (
        P(None, None, "dp", None),
        P(None, "section", None, None),
        P(None, "section", None),
        P(None, None, "dp", None),
    )
    out_specs = (P(None, "section", "dp", None), P(None, "section", "dp"))
    return jax.shard_map(on_device, mesh=mesh, in_specs=in_specs, out_specs=out_specs, check_vma=False)
```

time: 112 us -> 89.2 us (0.80)
  Pallas kernels: 107 us -> 84.9 us
    pallas_call x1, Pallas kernels: 107 us -> 84.9 us  [on_device(): pl.pallas_call(kernel, out_shape=(jax.ShapeDtypeStruct((2, 16, C), BF16),...]
where the time goes in v2:
time: 89.2 us; the launch traced here: 88.2 us
  Pallas kernels  84.9 us (95%)
  local copies, waits for them, and re-layouts  2.67 us (3%)
    pallas_call x1, Pallas kernels, on_device(): pl.pallas_call(kernel, out_shape=(jax.ShapeDtypeStruct((2, 16, C), BF16),...  84.9 us
    unnamed x2, local copies, waits for them, and re-layouts  2.67 us

profile of v2, /device:TPU:2, one launch (start us, length us, event | category | flops | bytes accessed | tf_op | source)
XLA Modules:
  0.0 88.2 jit_solution(8215571035935783388)
XLA Ops:
  0.6 84.9 %relay.1 = (bf16[2,16,1024]{2,1,0:T(8,128)(2,1)}, f32[2,16]{1,0:T(2,128)}) custom-call(bf16[2,256,1024]{2,1,0:T(8,128)(2,1)} %bitcast.10, bf16[2,1024,1024]{2,1,0:T(8,128)(2,1)} %bitcast.9, f32[2,1,1024]{2,1,0:T(1,128)} %decay.1, bf16[2,256,1024]{2,1,0:T(8,128)(2,1)} %bitcast.11), custom_call_target="tpu_custom_call" | custom-call | tf_op jit(solution)/shard_map/relay/pallas_call | solution.py:468
  85.5 1.5 %copy.10 = bf16[2,1,16,1024]{3,2,1,0:T(8,128)(2,1)} copy(bf16[2,1,16,1024]{3,2,1,0:T(8,128)(2,1)} %bitcast.12) | data formatting | bytes 131072
  87.0 1.2 %copy.11 = f32[2,1,16]{2,1,0:T(1,128)} copy(f32[2,1,16]{2,1,0:T(1,128)} %bitcast.13) | data formatting | bytes 256

commit v3 on v2

--- a/solution.py
+++ b/solution.py
@@ -18,8 +18,10 @@
 GAIN = 4.0
 
 SUBS = 2
-WINDOW = 1
+WINDOW = 2
 UNIT = 64 // SUBS
+PLUS = ("y", "z", "y", "z", "xl", "xh", "xh", "xh")
+MINUS = ("z", "y", "z", "y", "xl", "xh", "xh", "xh")
 X, Y, Z, ZD, YD, XYD = "x", "y", "z", "zd", "yd", "xyd"
 
 STREAMS = (
@@ -38,11 +40,11 @@
     ),
 )
 ORDER = (
-    16, 17, -1, 18, 19, -1, -1, -1, 17, 17, -1, -1, -2, 0, 18, 1, -1, 3, 2, 17,
-    16, 19, 0, 0, 4, 17, 3, -2, 2, 2, 18, 16, 0, 17, 0, 1, 19, 2, 18, 18,
-    3, 2, 4, -2, 0, 16, 1, 19, 19, 17, 3, 3, 18, 18, 2, 4, 16, 19, 0, 3,
-    16, 3, 19, 18, 1, 16, 19, 3, 0, -2, 16, 2, 4, 16, 0, 17, 3, 18, 19, 1,
-    0, 16, 2, 3, 17, 18, 19, 4,
+    16, 17, -1, 18, 19, -1, -1, -1, 17, 17, -1, -1, -2, 0, 1, -1, 3, 18, 2, 4,
+    17, 17, 16, 0, 19, 0, 2, -2, 3, 2, 17, 16, 0, 18, 0, 1, 2, 19, 2, 17,
+    3, 0, 4, -2, 18, 18, 16, 1, 19, 2, 19, 17, 3, 3, 4, 16, 0, 19, 18, 18,
+    16, 1, 17, 3, 16, 2, 19, 0, 3, -2, 19, 4, 16, 18, 3, 16, 1, 19, 0, 2,
+    3, 16, 18, 4, 19, 0, 3, 18,
 )
 SIZES = {"x": 2, "y": NY, "z": NZ}
 
@@ -124,9 +126,9 @@
     colour_there = (4 * (1 - xl) + 2 * y + z) % 8
     colour = (4 * xl + 2 * y + z) % 8
 
-    def rows_of(half, sub, unit, low, count):
-        start = half * 512 + sub * (512 // SUBS) + (unit % 8) * UNIT + low
-        return pl.ds(pl.multiple_of(start, 16), count)
+    def rows_of(half, sub, unit):
+        start = half * 512 + sub * (512 // SUBS) + (unit % 8) * UNIT
+        return pl.ds(pl.multiple_of(start, 16), UNIT)
 
     dec_copies = []
     for i, to in enumerate((core, across(c), across(1 - c))):
@@ -135,62 +137,79 @@
         copy.start()
 
     def send_across(phase):
-        r, sub = divmod(phase, SUBS)
-        for piece, (unit, count) in enumerate(((0, UNIT), (3, UNIT // 2))):
+        if phase < 2:
             for half in range(2):
-                rows = rows_of(half, sub, colour_there + unit, 0, count)
-                remote(
-                    weights.at[r, rows], w.at[r * 4 + sec, rows], xh_s, pc_r.at[r * 2 + c, sub, piece], across(half)
-                ).start()
+                rows = rows_of(half, phase, colour_there)
+                remote(weights.at[0, rows], w.at[sec, rows], xh_s, pc_r.at[c, phase, 0], across(half)).start()
+            return
+        layer = 2 + xh * 2 + phase
+        for sub in range(2):
+            here = w.at[layer, rows_of(c, sub, colour_there)]
+            remote(here, here, xh_s, pc_r.at[phase, sub, 0], across(c)).start()
+        if phase == 3:
+            for i in range(4, 8):
+                for route, piece, unit in ((PLUS, 1, 3), (MINUS, 7, 5)):
+                    if route[i] == "xh":
+                        here = w.at[2 + xh * 2 + i // 2, rows_of(c, i % 2, colour_there + unit)]
+                        remote(here, here, xh_s, pc_r.at[i // 2, i % 2, piece], across(c)).start()
 
     for phase in range(WINDOW):
         send_across(phase)
     remote(weights.at[0], w.at[sec], cw_s.at[0], cw_r.at[0], core).start()
+    remote(weights.at[1], w.at[4 + sec], cw_s.at[1], cw_r.at[1], core).start()
 
     def layer_of(q):
         return (q // 2) * 4 + (1 - xh) * 2 + q % 2
 
-    low_half, high_half = (0, UNIT // 2), (UNIT // 2, UNIT // 2)
-    every = (0, UNIT)
-    PIECES = (
-        (0, *every), (3, *low_half), (1, *every), (7, *every), (2, *every), (6, *every), (4, *every),
-        (3, *high_half), (5, *low_half), (5, *high_half),
-    )
-
-    def pass_on(q, sub, unit, low, count, piece, to):
-        here = w.at[layer_of(q), rows_of(c, sub, colour + unit, low, count)]
+    PIECES = (0, 3, 1, 7, 2, 6, 4, 5)
+
+    def pass_on(q, sub, unit, piece, to):
+        here = w.at[layer_of(q), rows_of(c, sub, colour + unit)]
         remote(here, here, gs.at[q], pc_r.at[q, sub, piece], to).start()
 
     def arrived(q, sub, piece):
-        unit, low, count = PIECES[piece]
-        here = w.at[layer_of(q), rows_of(c, sub, colour + unit, low, count)]
+        here = w.at[layer_of(q), rows_of(c, sub, colour + PIECES[piece])]
         pltpu.make_async_copy(here, here, pc_r.at[q, sub, piece]).wait()
 
     def both(phase):
-        lap, sub = divmod(phase, SUBS)
-        return ((lap * 2, sub), (lap * 2 + 1, sub))
+        return ((0, phase), (1, phase)) if phase < 2 else ((phase, 0), (phase, 1))
 
     def first_hop(phase):
         for q, sub in both(phase):
             arrived(q, sub, 0)
             for piece, to in ((4, y_by(3)), (5, y_by(1)), (6, to_xl), (3, z_by(1)), (2, z_by(7))):
-                pass_on(q, sub, 0, *every, piece, to)
+                pass_on(q, sub, 0, piece, to)
+        if phase == 0:
+            local[1].wait()
+            pltpu.make_async_copy(w.at[4], w.at[4], cw_r.at[1]).wait()
         if phase + WINDOW < 2 * SUBS:
             send_across(phase + WINDOW)
-        if phase == SUBS - 1:
-            remote(weights.at[1], w.at[4 + sec], cw_s.at[1], cw_r.at[1], core).start()
 
     def second_hop(phase):
-        for q, sub in both(phase):
+        for i, (q, sub) in enumerate(both(phase)):
+            plus, minus = PLUS[phase * 2 + i], MINUS[phase * 2 + i]
             arrived(q, sub, 2)
-            pass_on(q, sub, 1, *high_half, 7, y_by(3))
-            pass_on(q, sub, 1, *high_half, 9, to_xl)
+            if plus == "y":
+                pass_on(q, sub, 1, 1, y_by(3))
+            if minus == "xl":
+                pass_on(q, sub, 1, 7, to_xl)
             arrived(q, sub, 3)
-            pass_on(q, sub, 7, *low_half, 8, y_by(1))
+            if minus == "y":
+                pass_on(q, sub, 7, 7, y_by(1))
+            if plus == "xl":
+                pass_on(q, sub, 7, 1, to_xl)
+            if plus == "z":
+                arrived(q, sub, 4)
+                pass_on(q, sub, 2, 1, z_by(7))
+            if minus == "z":
+                arrived(q, sub, 5)
+                pass_on(q, sub, 6, 7, z_by(1))
 
     def rest(phase):
-        for q, sub in both(phase):
-            for piece in (1, 4, 5, 6, 7, 8, 9):
+        for i, (q, sub) in enumerate(both(phase)):
+            for piece in (4, 5, 6, 1, 7):
+                if (piece == 4 and PLUS[phase * 2 + i] == "z") or (piece == 5 and MINUS[phase * 2 + i] == "z"):
+                    continue
                 arrived(q, sub, piece)
             start = c * 512 + sub * (512 // SUBS)
             here = w.at[layer_of(q), pl.ds(pl.multiple_of(start, 128), 512 // SUBS)]
@@ -205,13 +224,16 @@
     def forward(layer):
         lap = layer // 4
 
-        @pl.when(own_chip(layer) & (layer % 2 == c))
+        @pl.when(own_chip(layer) & (layer % 2 == c) & (lap == 0))
         def _():
-            pltpu.make_async_copy(weights.at[lap], w.at[layer], l_sem.at[lap]).wait()
+            pltpu.make_async_copy(weights.at[0], w.at[layer], l_sem.at[0]).wait()
+
+        @pl.when(own_chip(layer) & (layer % 2 != c) & (lap == 0))
+        def _():
+            pltpu.make_async_copy(w.at[layer], w.at[layer], cw_r.at[0]).wait()
 
         @pl.when(own_chip(layer) & (layer % 2 != c))
         def _():
-            pltpu.make_async_copy(w.at[layer], w.at[layer], cw_r.at[lap]).wait()
             remote(act.at[layer], p_act.at[lap], pa_s.at[lap], pa_r.at[lap], core).start()
 
         @pl.when(jnp.logical_not(own_chip(layer)))
@@ -370,7 +392,7 @@
             for k in range(n - 1):
                 total = total + buffer[k]
             dv[...] = total
-        gd_ref[...] = pltpu.roll(dv[...], (C - dp * 16) % C, axis=1)[:, :16]
+        gd_ref[...] = pltpu.roll(dv[...], (C - dp * 16) % C, axis=1)
 
     start = 2 - 2 * xh
     local[2].wait()
@@ -386,18 +408,22 @@
         lax.fori_loop(low, high, body, 0)
 
     forward_loop(0, start)
-    done = 0
-    for step in range(2 * SUBS + 2):
-        if step < 2 * SUBS:
-            first_hop(step)
-        if 0 <= step - 1 < 2 * SUBS:
-            second_hop(step - 1)
-        if step - 2 >= 0:
-            rest(step - 2)
-        if SUBS + 1 <= step < 2 * SUBS + 1 and done < 4:
-            forward(start + done)
-            done += 1
-    forward_loop(start + done, 8)
+    first_hop(0)
+    first_hop(1)
+    second_hop(0)
+    first_hop(2)
+    second_hop(1)
+    rest(0)
+    first_hop(3)
+    second_hop(2)
+    rest(1)
+    forward(start)
+    forward(start + 1)
+    second_hop(3)
+    rest(2)
+    forward(start + 2)
+    rest(3)
+    forward_loop(start + 3, 8)
 
     local[3].wait()
     count = 4 - 2 * xh
@@ -428,16 +454,24 @@
         copy.wait_send()
     for copy in dec_copies:
         copy.wait_send()
-    sent = w.at[0, pl.ds(0, 384)]
+    direct = sum(route[i] == "xh" for route in (PLUS, MINUS) for i in range(8))
+    sent = w.at[0, pl.ds(0, (8 + direct) * UNIT)]
     pltpu.make_async_copy(sent, sent, xh_s).wait()
     for q in range(4):
-        sent = w.at[0, pl.ds(0, 928)]
+        parts = (q, q + 2) if q < 2 else (2 * q, 2 * q + 1)
+        passed = sum(5 + (PLUS[p] != "xh") + (MINUS[p] != "xh") for p in parts)
+        sent = w.at[0, pl.ds(0, passed * UNIT + 512)]
         pltpu.make_async_copy(sent, sent, gs.at[q]).wait()
     for r in range(2):
         pltpu.make_async_copy(w.at[0], w.at[0], cw_s.at[r]).wait()
         pltpu.make_async_copy(p_act.at[r], p_act.at[r], pa_s.at[r]).wait()
         pltpu.make_async_copy(p_gq.at[r], p_gq.at[r], pg_s.at[r]).wait()
         pltpu.make_async_copy(dd_in.at[r], dd_in.at[r], dd_s.at[r]).wait()
+
+
+def hand_on(gw_in, gd_in, gw_ref, gd_ref):
+    gw_ref[...] = gw_in[...]
+    gd_ref[...] = gd_in[:, :16]
 
 
 def on_device(currents, weights, decay, out_grad):
@@ -459,7 +493,7 @@
         vmem((NY - 1, 2, C), F32),
         vmem((NZ - 1, 2, C), F32),
         vmem((1, 2, C), F32),
-        dma((5,)), dma((2, 3)), dma((2,)), dma((2,)), dma, dma((4, SUBS, 10)), dma((4,)), dma((4, SUBS)),
+        dma((5,)), dma((2, 3)), dma((2,)), dma((2,)), dma, dma((4, SUBS, 8)), dma((4,)), dma((4, SUBS)),
         dma((2,)), dma((2,)), dma((2,)), dma((2,)), dma((2,)), dma((2,)), dma((24,)), dma((24,)),
         dma((len(KEYS),)), dma((len(KEYS),)),
     ] + [vmem(PLAN[key], BF16) for key in KEYS]
@@ -467,7 +501,7 @@
     in_vmem = pl.BlockSpec(memory_space=pltpu.VMEM)
     gw, gd = pl.pallas_call(
         kernel,
-        out_shape=(jax.ShapeDtypeStruct((2, 16, C), BF16), jax.ShapeDtypeStruct((2, 16), F32)),
+        out_shape=(jax.ShapeDtypeStruct((2, 16, C), BF16), jax.ShapeDtypeStruct((2, C), F32)),
         in_specs=[anywhere] * 4,
         out_specs=(in_vmem, in_vmem),
         scratch_shapes=scratch,
@@ -481,6 +515,13 @@
         decay,
         out_grad.reshape(2, ROWS, C),
     )
+    gw, gd = pl.pallas_call(
+        hand_on,
+        out_shape=(jax.ShapeDtypeStruct((2, 16, C), BF16), jax.ShapeDtypeStruct((2, 16), F32)),
+        in_specs=[in_vmem] * 2,
+        out_specs=(in_vmem, in_vmem),
+        name="results",
+    )(gw, gd)
     return gw[:, None], gd[:, None]
 
 

time: 89.2 us -> 85.9 us (0.963); the launches traced: 88.2 us -> 85.8 us
  local copies, waits for them, and re-layouts: 2.67 us -> 0 us
    unnamed x2 -> x0, local copies, waits for them, and re-layouts: 2.67 us -> none
    pallas_call x0 -> x1, Pallas kernels: none -> 1.48 us  [on_device(): pl.pallas_call(hand_on, out_shape=(jax.ShapeDtypeStruct((2, 16, C), BF16)...]
    pallas_call x1, Pallas kernels: 84.9 us -> 83.7 us  [on_device(): pl.pallas_call(kernel, out_shape=(jax.ShapeDtypeStruct((2, 16, C), BF16),...]
where the time goes in v3:
time: 85.9 us; the launch traced here: 85.8 us
  Pallas kernels  85.2 us (99%)
    pallas_call x1, Pallas kernels, on_device(): pl.pallas_call(kernel, out_shape=(jax.ShapeDtypeStruct((2, 16, C), BF16),...  83.7 us

profile of v3, /device:TPU:2, one launch (start us, length us, event | category | flops | bytes accessed | tf_op | source)
XLA Modules:
  0.0 85.8 jit_solution(18390157477811822216)
XLA Ops:
  0.6 83.7 %relay.1 = (bf16[2,16,1024]{2,1,0:T(8,128)(2,1)}, f32[2,1024]{1,0:T(2,128)}) custom-call(bf16[2,256,1024]{2,1,0:T(8,128)(2,1)} %bitcast.10, bf16[2,1024,1024]{2,1,0:T(8,128)(2,1)} %bitcast.9, f32[2,1,1024]{2,1,0:T(1,128)} %decay.1, bf16[2,256,1024]{2,1,0:T(8,128)(2,1)} %bitcast.11), custom_call_target="tpu_custom_call" | custom-call | tf_op jit(solution)/shard_map/relay/pallas_call | solution.py:502
  84.3 1.5 %results.1 = (bf16[2,16,1024]{2,1,0:T(8,128)(2,1)}, f32[2,16]{1,0:T(2,128)}) custom-call(bf16[2,16,1024]{2,1,0:T(8,128)(2,1)} %get-tuple-element.6.gw_in, f32[2,1024]{1,0:T(2,128)} %get-tuple-element.7.gd_in), custom_call_target="tpu_custom_call" | custom-call | tf_op jit(solution)/shard_map/results/pallas_call | solution.py:518

commit v4 on v3

--- a/solution.py
+++ b/solution.py
@@ -243,9 +243,9 @@
                 here = w.at[layer, pl.ds(pl.multiple_of(start, 128), 512 // SUBS)]
                 pltpu.make_async_copy(here, here, half_r.at[lap * 2 + layer % 2, sub]).wait()
 
-        @pl.loop(0, 4, unroll=True)
+        @pl.loop(0, 2, unroll=True)
         def _(j):
-            cols = tile(j)
+            cols = tile(j, 512)
             pre = jnp.dot(act[layer], w[layer, :, cols], preferred_element_type=F32)
             rate = dec[layer % 4, lap, :, cols]
             old = act[layer, :, cols].astype(F32)

time: 85.9 us -> 84.6 us (0.985)
  Pallas kernels: 85.2 us -> 83.9 us
    pallas_call x1, Pallas kernels: 83.7 us -> 82.4 us  [on_device(): pl.pallas_call(kernel, out_shape=(jax.ShapeDtypeStruct((2, 16, C), BF16),...]
where the time goes in v4:
time: 84.6 us; the launch traced here: 84.5 us
  Pallas kernels  83.9 us (99%)
    pallas_call x1, Pallas kernels, on_device(): pl.pallas_call(kernel, out_shape=(jax.ShapeDtypeStruct((2, 16, C), BF16),...  82.4 us

profile of v4, /device:TPU:2, one launch (start us, length us, event | category | flops | bytes accessed | tf_op | source)
XLA Modules:
  0.0 84.5 jit_solution(15743231684957663529)
XLA Ops:
  0.6 82.4 %relay.1 = (bf16[2,16,1024]{2,1,0:T(8,128)(2,1)}, f32[2,1024]{1,0:T(2,128)}) custom-call(bf16[2,256,1024]{2,1,0:T(8,128)(2,1)} %bitcast.10, bf16[2,1024,1024]{2,1,0:T(8,128)(2,1)} %bitcast.9, f32[2,1,1024]{2,1,0:T(1,128)} %decay.1, bf16[2,256,1024]{2,1,0:T(8,128)(2,1)} %bitcast.11), custom_call_target="tpu_custom_call" | custom-call | tf_op jit(solution)/shard_map/relay/pallas_call | solution.py:502
  83.0 1.5 %results.1 = (bf16[2,16,1024]{2,1,0:T(8,128)(2,1)}, f32[2,16]{1,0:T(2,128)}) custom-call(bf16[2,16,1024]{2,1,0:T(8,128)(2,1)} %get-tuple-element.6.gw_in, f32[2,1024]{1,0:T(2,128)} %get-tuple-element.7.gd_in), custom_call_target="tpu_custom_call" | custom-call | tf_op jit(solution)/shard_map/results/pallas_call | solution.py:518

commit v5 on v4

--- a/solution.py
+++ b/solution.py
@@ -300,16 +300,16 @@
         over_rows = (((0,), (0,)), ((), ()))
         cols = pl.ds(n * 512, 512)
 
-        @pl.loop(0, 4, unroll=True)
+        @pl.loop(0, 2, unroll=True)
         def _(i):
             total = lax.dot_general(
-                act[layer, :, tile(i)], gq[layer, :, cols], over_rows, preferred_element_type=F32
+                act[layer, :, tile(i, 512)], gq[layer, :, cols], over_rows, preferred_element_type=F32
             ) + lax.dot_general(
-                p_act[lap, :, tile(i)], p_gq[lap, :, cols], over_rows, preferred_element_type=F32
+                p_act[lap, :, tile(i, 512)], p_gq[lap, :, cols], over_rows, preferred_element_type=F32
             )
             for b in range(4):
-                block = total[:, b * 128 : (b + 1) * 128].astype(BF16).reshape(2, 8, 16, 128)
-                part[lap, n * 4 + b, i // 2, pl.ds((i % 2) * 2, 2)] = block
+                block = total[:, b * 128 : (b + 1) * 128].astype(BF16).reshape(4, 8, 16, 128)
+                part[lap, n * 4 + b, i] = block
 
     sums = []
 

time: 84.6 us -> 84.6 us (level)
  no operation moved by 1% of the time
where the time goes in v5:
time: 84.6 us; the launch traced here: 84.5 us
  Pallas kernels  83.9 us (99%)
    pallas_call x1, Pallas kernels, on_device(): pl.pallas_call(kernel, out_shape=(jax.ShapeDtypeStruct((2, 16, C), BF16),...  82.4 us

profile of v5, /device:TPU:2, one launch (start us, length us, event | category | flops | bytes accessed | tf_op | source)
XLA Modules:
  0.0 84.5 jit_solution(16032944449761683906)
XLA Ops:
  0.6 82.4 %relay.1 = (bf16[2,16,1024]{2,1,0:T(8,128)(2,1)}, f32[2,1024]{1,0:T(2,128)}) custom-call(bf16[2,256,1024]{2,1,0:T(8,128)(2,1)} %bitcast.10, bf16[2,1024,1024]{2,1,0:T(8,128)(2,1)} %bitcast.9, f32[2,1,1024]{2,1,0:T(1,128)} %decay.1, bf16[2,256,1024]{2,1,0:T(8,128)(2,1)} %bitcast.11), custom_call_target="tpu_custom_call" | custom-call | tf_op jit(solution)/shard_map/relay/pallas_call | solution.py:502
  83.0 1.5 %results.1 = (bf16[2,16,1024]{2,1,0:T(8,128)(2,1)}, f32[2,16]{1,0:T(2,128)}) custom-call(bf16[2,16,1024]{2,1,0:T(8,128)(2,1)} %get-tuple-element.6.gw_in, f32[2,1024]{1,0:T(2,128)} %get-tuple-element.7.gd_in), custom_call_target="tpu_custom_call" | custom-call | tf_op jit(solution)/shard_map/results/pallas_call | solution.py:518
